TPU v7x, 128 devices: a whole 4x4x4 slice. The times are simulated.
128 devices in a mesh: sx: 16 (over z, y), sy: 8 (over x, core).
Axes of the slice: x: 4, y: 4, z: 4, core: 2. Of those that a mesh axis runs over, the one named last changes fastest.
Arguments:
- control: float32 [2, 127, 256, 1024], P(None, None, 'sx', 'sy'), may hold values from -6 to 6
- deviation: float32 [2, 127, 256, 1024], P(None, None, 'sx', 'sy'), may hold values from 0.3 to 3
- vertical: float32 [2, 127, 127], replicated, may hold values from -0.5 to 0.5
- length: float32 [2, 127], replicated, may hold values from 1.5 to 6
- owners: int32 [254, 1], replicated, may hold values from 0 to 127; in each aligned block of 254 rows (0 to 253, 254 to 507, ...) at most 4 rows name the same one
Outputs:
- result: float32 [2, 127, 256, 1024], P(None, None, 'sx', 'sy')
- slab_fields: float32 [128, 4, 256, 1024], P(('sx', 'sy'))
Inputs may be any that keep to these rules, and one draw needn't show every extreme that they name: `owners`: each device owns at most 4 slabs and some device owns exactly 4.
All inputs are finite; a program needn't handle non-finite values.
Results may differ from a plain program's by a relative error of at most 0.000071.
Values sent between devices are 32-bit elements; how exact they have to be, the bound alone decides.
A program may use at most 320 MiB of HBM per device.

v0:
```python
import jax
import jax.numpy as jnp
from jax import lax
from jax.experimental import pallas as pl
from jax.experimental.pallas import tpu as pltpu
from jax.sharding import PartitionSpec as P

MESH = pl.DeviceIdType.MESH
BAND = 12
VARS, LEV, ROWS, COLS = 2, 127, 16, 128
SX, SY = 16, 8
DEVICES = SX * SY
VMEM_LIMIT = 57 * 2**20
SETTLE_LIMIT = 103 * 2**19
NLON, NLAT = 256, 1024
PLACES = 2 * DEVICES
LIFT = VARS * LEV * ROWS


def split(x):
    high = x.astype(jnp.bfloat16)
    return high, (x - high.astype(jnp.float32)).astype(jnp.bfloat16)


def dot(a, b):
    return jnp.dot(a, b, preferred_element_type=jnp.float32)


def dot3(a, b):
    return dot(a[0], b[0]) + (dot(a[0], b[1]) + dot(a[1], b[0]))


def where_to(owner_col, owner_row, label):
    shape = (PLACES, PLACES)
    down = lax.broadcasted_iota(jnp.int32, shape, 0).astype(jnp.float32)
    over = lax.broadcasted_iota(jnp.int32, shape, 1).astype(jnp.float32)
    one = lambda c: jnp.where(c, 1.0, 0.0)
    device_col, device_row = jnp.floor(label / 2.0), jnp.floor(over[:1] / 2.0)
    count_col = jnp.sum(one(owner_row == device_col), axis=1, keepdims=True)
    count_row = jnp.sum(one(owner_col == device_row), axis=0, keepdims=True)
    taken_col = one(count_col > label - 2.0 * device_col)
    taken_row = one(count_row > over[:1] - 2.0 * device_row)
    free_rank_col = jnp.sum((1.0 - taken_row) * one(over < label), axis=1, keepdims=True)
    same = one(owner_col == owner_row)
    above = one(down < over)
    slot_row = jnp.sum(same * above, axis=0, keepdims=True)
    slot_col = jnp.sum(same * one(over < down), axis=1, keepdims=True)
    extra_row = one(owner_row >= 0.0) * one(slot_row >= 2.0)
    extra_col = one(owner_col >= 0.0) * one(slot_col >= 2.0)
    place_row = 2.0 * owner_row + slot_row
    rank_row = jnp.sum(extra_col * above, axis=0, keepdims=True)
    native = one(label == jnp.where(owner_row >= 0.0, place_row, -1.0)) * (1.0 - extra_row)
    lent = one(free_rank_col == rank_row) * extra_row * (1.0 - taken_col)
    extra = one(label == place_row - 2.0) * extra_row
    return native + lent, extra, taken_col


def smooth_matrices(long, lon, lat):
    lane = lax.broadcasted_iota(jnp.int32, (8, COLS), 1)
    offset = (lane - BAND).astype(jnp.float32)
    bell = jnp.where(lane <= 2 * BAND, jnp.exp(-(offset * offset) / (2.0 * long * long)), 0.0)
    norm = jnp.sqrt(jnp.sum(bell * bell, axis=1, keepdims=True))[0:1, :]

    def weigh(d):
        near = (d >= -BAND) & (d <= BAND)
        d = d.astype(jnp.float32)
        return jnp.where(near, jnp.exp(-(d * d) / (2.0 * long * long)) / norm, 0.0)

    shape = (NLON, NLON)
    d = lax.broadcasted_iota(jnp.int32, shape, 1) - lax.broadcasted_iota(jnp.int32, shape, 0)
    d = jnp.where(d >= NLON // 2, d - NLON, jnp.where(d < -(NLON // 2), d + NLON, d))
    lon[0], lon[1] = split(weigh(d))
    shape = (512, 256)
    d = lax.broadcasted_iota(jnp.int32, shape, 0) - 128 - lax.broadcasted_iota(jnp.int32, shape, 1)
    lat[0], lat[1] = split(weigh(d))


def travel_kernel(
    control_hbm, deviation_hbm, vertical_hbm, length_hbm, owners_hbm,
    returned, field_hbm,
    control, deviation, vertical_ref, length_ref, owners_ref, scaled, pieces, matrix, length_row_ref,
    home, extra, outgoing, along, lon, lat, field, back,
    in_sem, send_sem, home_sem, extra_sem, back_sem, own_sem, out_sem, column_sem,
):
    mx, my = lax.axis_index("sx"), lax.axis_index("sy")
    me = mx * SY + my
    here = my * SX + mx
    z, y, x, core = mx // 4, mx % 4, my // 2, my % 2

    def partner(step):
        k = DEVICES - step
        px = ((z + (k // 4) % 4) % 4) * 4 + (y + (k // 16) % 4) % 4
        py = ((x + k % 4) % 4) * 2 + (core + k // 64) % 2
        return px, py

    barrier = pltpu.get_barrier_semaphore()

    @pl.loop(1, SX)
    def _(step):
        pl.semaphore_signal(barrier, inc=1, device_id=(lax.rem(mx + step, SX), my), device_id_type=MESH)

    @pl.loop(1, SY)
    def _(step):
        pl.semaphore_signal(barrier, inc=1, device_id=(mx, lax.rem(my + step, SY)), device_id_type=MESH)

    cut = LIFT // 2
    small = []
    for at, (src, dst) in enumerate(
        ((owners_hbm, owners_ref), (vertical_hbm, vertical_ref), (length_hbm, length_ref))
    ):
        small.append(pltpu.make_async_copy(src, dst, in_sem.at[4 + at]))
        small[-1].start()
    loads = []
    for part in range(2):
        rows = pl.ds(part * cut, cut)
        for at, (src, dst) in enumerate(((control_hbm, control), (deviation_hbm, deviation))):
            loads.append(pltpu.make_async_copy(src.at[rows], dst.at[rows], in_sem.at[2 * part + at]))
    for load in loads:
        load.start()

    control[LIFT:, :] = jnp.zeros((ROWS, COLS), jnp.float32)
    deviation[LIFT:, :] = jnp.zeros((ROWS, COLS), jnp.float32)
    length_row_ref[...] = jnp.ones((1, PLACES), jnp.float32)
    matrix[...] = jnp.zeros((PLACES, PLACES), jnp.float32)
    for load in small:
        load.wait()
    for v in range(VARS):
        length_row_ref[:, v * 128 : v * 128 + LEV] = length_ref[v : v + 1, :]
        matrix[v * 128 : v * 128 + LEV, v * 128 : v * 128 + LEV] = vertical_ref[:, v, :]
    slab = lax.broadcasted_iota(jnp.int32, (PLACES, VARS * LEV), 0)
    level = slab % 128
    number = jnp.where(level < LEV, slab - slab // 128, -1)
    listed = lax.broadcasted_iota(jnp.int32, (PLACES, VARS * LEV), 1) == number
    owners = owners_ref[...].astype(jnp.float32)
    owner_col = jnp.sum(jnp.where(listed, owners + 1.0, 0.0), axis=1, keepdims=True) - 1.0
    shape = (PLACES, PLACES)
    down = lax.broadcasted_iota(jnp.int32, shape, 0)
    over = lax.broadcasted_iota(jnp.int32, shape, 1)
    owner_row = jnp.sum(jnp.where(down == over, owner_col, 0.0), axis=0, keepdims=True)
    row = lax.broadcasted_iota(jnp.int32, (PLACES, 1), 0)
    side = jnp.where(row < DEVICES, 1 - core, core)
    label = (4 * ((row % DEVICES) // 2) + 2 * side + row % 2).astype(jnp.float32)
    home_hot, extra_hot, taken_col = where_to(owner_col, owner_row, label)
    high, low = split(matrix[...])

    def lift(hot, first):
        hot = hot.astype(jnp.bfloat16)
        rows = (dot(hot, high).astype(jnp.bfloat16), dot(hot, low).astype(jnp.bfloat16))
        for i in range(0, ROWS, 2):
            lifted = dot3(rows, (scaled[0, i // 2], scaled[1, i // 2]))
            for r in (0, 1):
                at = pl.ds(first * ROWS + i + r, hot.shape[0], stride=ROWS)
                pieces[at, :] = lifted[:, r * COLS : (r + 1) * COLS]

    def seat(px, py, other_core):
        return jnp.where(py % 2 == other_core, DEVICES, 0) + 2 * (px * 4 + py // 2)

    def two(first, px, py):
        return pieces.at[pl.ds((first + seat(px, py, core)) * ROWS, 2 * ROWS)]

    def scatter(first, into, sem, begin, end):
        @pl.loop(begin, end)
        def _(step):
            px, py = partner(step)
            pltpu.make_async_remote_copy(
                src_ref=two(first, px, py),
                dst_ref=into.at[here],
                send_sem=send_sem,
                recv_sem=sem,
                device_id=(px, py),
                device_id_type=MESH,
            ).start()

    pl.semaphore_wait(barrier, SX + SY - 2)

    @pl.loop(1, SY)
    def _(step):
        pl.semaphore_signal(column_sem, inc=1, device_id=(mx, lax.rem(my + step, SY)), device_id_type=MESH)

    for load in loads:
        load.wait()
    for i in range(0, ROWS, 2):
        sides = []
        for r in (i, i + 1):
            halves = []
            for v in range(VARS):
                at = pl.ds(v * LEV * ROWS + r, 128, stride=ROWS)
                halves.append(control[at, :] * deviation[at, :])
            sides.append(jnp.concatenate(halves, axis=0))
        scaled[0, i // 2], scaled[1, i // 2] = split(jnp.concatenate(sides, axis=1))

    lift(home_hot[:DEVICES], 0)
    pl.semaphore_wait(column_sem, SY - 1)
    scatter(0, home, home_sem, 1, DEVICES // 2 + 1)
    lift(home_hot[DEVICES:], DEVICES)
    scatter(0, home, home_sem, DEVICES // 2 + 1, DEVICES)
    own_home = pltpu.make_async_copy(two(0, mx, my), home.at[here], own_sem.at[0])
    own_home.start()
    lift(extra_hot, PLACES)
    scatter(PLACES, extra, extra_sem, 1, DEVICES)
    own_extra = pltpu.make_async_copy(two(PLACES, mx, my), extra.at[here], own_sem.at[1])
    own_extra.start()

    turned_high, turned_low = split(matrix[...].T)
    home_turned = home_hot.T.astype(jnp.bfloat16)
    whole = dot(turned_high, home_turned) + dot(turned_low, home_turned)
    for side in range(2):
        back[side * PLACES : (side + 1) * PLACES, :] = whole[:, side * COLS : (side + 1) * COLS]
    out = [pltpu.make_async_copy(back, returned.at[pl.ds(PLACES * ROWS, 2 * PLACES)], out_sem.at[4])]
    out[0].start()
    length_row = length_row_ref[...]
    owned = []
    for at, hot in ((0, home_hot), (2, extra_hot)):
        used = jnp.sum(hot, axis=1, keepdims=True)
        long = jnp.sum(hot * length_row, axis=1, keepdims=True) + (1.0 - used)
        for h in range(2):
            mine = jnp.where(label == (2 * me + h).astype(jnp.float32), 1.0, 0.0)
            smooth_matrices(jnp.sum(mine * long, axis=0, keepdims=True), lon.at[at + h], lat.at[at + h])
            if at == 0:
                owned.append(jnp.sum(mine * taken_col, axis=0, keepdims=True))

    def smooth(h, source, keep):
        for t in range(4):
            blocks = [
                source[pl.ds((2 * t + b) * SX, SX), h * ROWS : (h + 1) * ROWS].reshape(NLON, COLS) for b in range(2)
            ]
            lifted = split(jnp.concatenate(blocks, axis=1))
            along[:, t * 256 : (t + 1) * 256] = dot3((lon[keep, 0], lon[keep, 1]), lifted)
        for t in range(4):
            begin, end = max(0, 256 * t - 128), min(NLAT, 256 * t + 384)
            taps = pl.ds(begin - (256 * t - 128), end - begin)
            done = dot3(split(along[:, begin:end]), (lat[keep, 0, taps, :], lat[keep, 1, taps, :]))
            if keep < 2:
                field[keep, :, t * 256 : (t + 1) * 256] = done * owned[keep]
                for b in range(2):
                    outgoing[pl.ds((2 * t + b) * SX, SX), h * ROWS : (h + 1) * ROWS] = done[
                        :, b * COLS : (b + 1) * COLS
                    ].reshape(SX, ROWS, COLS)
            else:
                field[keep, :, t * 256 : (t + 1) * 256] = done

    own_home.wait()
    pltpu.make_async_copy(home.at[pl.ds(0, DEVICES - 1)], home.at[pl.ds(0, DEVICES - 1)], home_sem).wait()
    for h in range(2):
        smooth(h, home, h)

    def into(other_core):
        return returned.at[pl.ds(ROWS * seat(mx, my, other_core), 2 * ROWS)]

    own_back = pltpu.make_async_copy(outgoing.at[here], into(core), own_sem.at[2])
    own_back.start()

    @pl.loop(1, DEVICES)
    def _(step):
        px, py = partner(step)
        pltpu.make_async_remote_copy(
            src_ref=outgoing.at[py * SX + px],
            dst_ref=into(py % 2),
            send_sem=send_sem,
            recv_sem=back_sem,
            device_id=(px, py),
            device_id_type=MESH,
        ).start()

    def write(h):
        out.append(pltpu.make_async_copy(field.at[h], field_hbm.at[h], out_sem.at[h]))
        out[-1].start()

    for h in range(2):
        write(h)
    own_extra.wait()
    pltpu.make_async_copy(extra.at[pl.ds(0, DEVICES - 1)], extra.at[pl.ds(0, DEVICES - 1)], extra_sem).wait()
    for h in range(2):
        smooth(h, extra, 2 + h)
        write(2 + h)
    own_back.wait()
    for copy in out:
        copy.wait()
    arrived = returned.at[pl.ds(0, 2 * ROWS * (DEVICES - 1))]
    pltpu.make_async_copy(arrived, arrived, back_sem).wait()
    for _ in range(3):
        pltpu.make_async_copy(arrived, arrived, send_sem).wait()


def settle_kernel(
    returned_hbm, deviation_hbm, field_hbm,
    result_hbm, fields_hbm,
    returned, deviation, back, field, result, in_sem, out_sem,
):
    half = ROWS // 2
    tail = pl.ds(PLACES, 2 * PLACES // ROWS)
    loads = [pltpu.make_async_copy(returned_hbm.at[tail], back, in_sem.at[0])]
    for part in range(2):
        rows = pl.ds(part * half, half)
        at = 1 + 2 * part
        loads.append(pltpu.make_async_copy(returned_hbm.at[pl.ds(0, PLACES), rows], returned.at[part], in_sem.at[at]))
        loads.append(pltpu.make_async_copy(deviation_hbm.at[:, rows], deviation.at[part], in_sem.at[at + 1]))
    slots = [pltpu.make_async_copy(field_hbm.at[h], field.at[h], in_sem.at[5 + h]) for h in range(4)]
    for load in loads + slots:
        load.start()
    out = []

    def write(src, dst):
        out.append(pltpu.make_async_copy(src, dst, out_sem.at[len(out)]))
        out[-1].start()

    loads[0].wait()
    flat = back[...].reshape(2 * PLACES, COLS)
    ways = split(jnp.concatenate([flat[:PLACES], flat[PLACES:]], axis=1))
    for part in range(2):
        for load in loads[1 + 2 * part : 3 + 2 * part]:
            load.wait()
        arrived = returned.at[part].reshape(PLACES * half, COLS)
        spread = deviation.at[part].reshape(VARS * LEV * half, COLS)
        settled_to = result.at[part].reshape(VARS * LEV * half, COLS)
        for i in range(0, half, 2):
            sides = [arrived[pl.ds(i + r, PLACES, stride=half), :] for r in range(2)]
            settled = dot3(ways, split(jnp.concatenate(sides, axis=1)))
            for r in range(2):
                for v in range(VARS):
                    at = pl.ds(v * LEV * half + i + r, LEV, stride=half)
                    settled_to[at, :] = spread[at, :] * settled[v * 128 : v * 128 + LEV, r * COLS : (r + 1) * COLS]
            slot = part * 4 + i // 2 - 2
            if 0 <= slot < 4:
                slots[slot].wait()
                write(field.at[slot], fields_hbm.at[slot])
        write(result.at[part], result_hbm.at[:, pl.ds(part * half, half)])
    for copy in out:
        copy.wait()


def local(control, deviation, vertical, length, owners):
    f32, bf16 = jnp.float32, jnp.bfloat16
    hbm = pl.BlockSpec(memory_space=pl.ANY)
    dma = pltpu.SemaphoreType.DMA
    flat, square = (LIFT, COLS), (PLACES, PLACES)
    block = (DEVICES, 2 * ROWS, COLS)
    deviation = deviation.reshape(flat)
    returned, field = pl.pallas_call(
        travel_kernel,
        out_shape=[
            jax.ShapeDtypeStruct((PLACES * ROWS + 2 * PLACES, COLS), f32),
            jax.ShapeDtypeStruct((4, NLON, NLAT), f32),
        ],
        in_specs=[hbm] * 5,
        out_specs=[hbm] * 2,
        scratch_shapes=[
            pltpu.VMEM((LIFT + ROWS, COLS), f32),
            pltpu.VMEM((LIFT + ROWS, COLS), f32),
            pltpu.VMEM((LEV, VARS, LEV), f32),
            pltpu.VMEM((VARS, LEV), f32),
            pltpu.VMEM((1, VARS * LEV), jnp.int32),
            pltpu.VMEM((2, ROWS // 2, PLACES, 2 * COLS), bf16),
            pltpu.VMEM((2 * PLACES * ROWS, COLS), f32),
            pltpu.VMEM(square, f32),
            pltpu.VMEM((1, PLACES), f32),
            pltpu.VMEM(block, f32),
            pltpu.VMEM(block, f32),
            pltpu.VMEM(block, f32),
            pltpu.VMEM((NLON, NLAT), f32),
            pltpu.VMEM((4, 2, NLON, NLON), bf16),
            pltpu.VMEM((4, 2, 512, 256), bf16),
            pltpu.VMEM((4, NLON, NLAT), f32),
            pltpu.VMEM((2 * PLACES, COLS), f32),
            dma((7,)), dma, dma, dma, dma, dma((3,)), dma((5,)),
            pltpu.SemaphoreType.REGULAR,
        ],
        compiler_params=pltpu.CompilerParams(
            collective_id=0, has_side_effects=True, vmem_limit_bytes=VMEM_LIMIT
        ),
        name="travel",
    )(control.reshape(flat), deviation, vertical.transpose(1, 0, 2), length, owners.reshape(1, VARS * LEV))

    half = (2, VARS * LEV, ROWS // 2, COLS)
    result, fields = pl.pallas_call(
        settle_kernel,
        out_shape=[
            jax.ShapeDtypeStruct((VARS * LEV, ROWS, COLS), f32),
            jax.ShapeDtypeStruct((4, NLON, NLAT), f32),
        ],
        in_specs=[hbm] * 3,
        out_specs=[hbm] * 2,
        scratch_shapes=[
            pltpu.VMEM((2, PLACES, ROWS // 2, COLS), f32),
            pltpu.VMEM(half, f32),
            pltpu.VMEM((2 * PLACES // ROWS, ROWS, COLS), f32),
            pltpu.VMEM((4, NLON, NLAT), f32),
            pltpu.VMEM(half, f32),
            dma((9,)),
            dma((6,)),
        ],
        compiler_params=pltpu.CompilerParams(vmem_limit_bytes=SETTLE_LIMIT),
        name="settle",
    )(
        returned.reshape(PLACES + 2 * PLACES // ROWS, ROWS, COLS),
        deviation.reshape(VARS * LEV, ROWS, COLS),
        field,
    )
    return result.reshape(VARS, LEV, ROWS, COLS), fields.reshape(1, 4, NLON, NLAT)


def solution(mesh):
    return jax.shard_map(
        local,
        mesh=mesh,
        in_specs=(P(None, None, "sx", "sy"), P(None, None, "sx", "sy"), P(), P(), P()),
        out_specs=(P(None, None, "sx", "sy"), P(("sx", "sy"), None, None, None)),
        check_vma=False,
    )
```

profile of v0, /device:TPU:0, one launch (start us, length us, event | category | flops | bytes accessed | tf_op | source)
XLA Modules:
  0.0 88.0 jit_solution(1538329232229101251)
XLA Ops:
  0.6 0.0 copy-start
  0.6 82.5 %travel.1 = (f32[4608,128]{1,0:T(8,128)}, f32[4,256,1024]{2,1,0:T(8,128)}) custom-call(f32[4064,128]{1,0:T(8,128)} %bitcast.11, f32[4064,128]{1,0:T(8,128)} %bitcast.8, f32[127,2,127]{2,1,0:T(2,128)} %bitcast.12, f32[2,127]{1,0:T(2,128)} %length_hbm.1, s32[1,254]{1,0:T(1,128)} %bitcast.13), custom_call_target="tpu_custom_call" | custom-call | tf_op jit(solution)/shard_map/travel/pallas_call | solution.py:339
  83.1 0.0 copy-done
  83.1 4.8 %settle.1 = (f32[254,16,128]{2,1,0:T(8,128)}, f32[4,256,1024]{2,1,0:T(8,128)}) custom-call(f32[288,16,128]{2,1,0:T(8,128)} %bitcast.10, f32[254,16,128]{2,1,0:T(8,128)S(1)} %bitcast.9, f32[4,256,1024]{2,1,0:T(8,128)} %get-tuple-element.7.field_hbm), custom_call_target="tpu_custom_call" | custom-call | tf_op jit(solution)/shard_map/settle/pallas_call | solution.py:375
Async XLA Ops:
  0.6 82.5 %copy-start = (f32[2,127,16,128]{3,2,1,0:T(8,128)S(1)}, f32[2,127,16,128]{3,2,1,0:T(8,128)}, u32[]{:S(2)}) copy-start(f32[2,127,16,128]{3,2,1,0:T(8,128)} %param.6) | copy-start | bytes 6242308
where the time goes:
time: 88.1 us; the launch traced here: 88 us
  Pallas kernels  87.3 us (99%)
    pallas_call x1, Pallas kernels, local(): pl.pallas_call(travel_kernel, out_shape=[jax.ShapeDtypeStruct((PLACES * R...  82.5 us
    pallas_call x1, Pallas kernels, local(): pl.pallas_call(settle_kernel, out_shape=[jax.ShapeDtypeStruct((VARS * LEV...  4.84 us

commit v1 on v0

--- a/solution.py
+++ b/solution.py
@@ -89,7 +89,7 @@
 
     def partner(step):
         k = DEVICES - step
-        px = ((z + (k // 4) % 4) % 4) * 4 + (y + (k // 16) % 4) % 4
+        px = ((z + k // 16 + k // 4) % 4) * 4 + (y + k // 4) % 4
         py = ((x + k % 4) % 4) * 2 + (core + k // 64) % 2
         return px, py
 

time: 88.1 us -> 87.5 us (level)
  no operation moved by 1% of the time
where the time goes in v1:
time: 87.5 us; the launch traced here: 87.3 us
  Pallas kernels  86.7 us (99%)
    pallas_call x1, Pallas kernels, local(): pl.pallas_call(travel_kernel, out_shape=[jax.ShapeDtypeStruct((PLACES * R...  81.8 us
    pallas_call x1, Pallas kernels, local(): pl.pallas_call(settle_kernel, out_shape=[jax.ShapeDtypeStruct((VARS * LEV...  4.84 us

profile of v1, /device:TPU:0, one launch (start us, length us, event | category | flops | bytes accessed | tf_op | source)
XLA Modules:
  0.0 87.3 jit_solution(7594200965951399168)
XLA Ops:
  0.6 0.0 copy-start
  0.6 81.8 %travel.1 = (f32[4608,128]{1,0:T(8,128)}, f32[4,256,1024]{2,1,0:T(8,128)}) custom-call(f32[4064,128]{1,0:T(8,128)} %bitcast.11, f32[4064,128]{1,0:T(8,128)} %bitcast.8, f32[127,2,127]{2,1,0:T(2,128)} %bitcast.12, f32[2,127]{1,0:T(2,128)} %length_hbm.1, s32[1,254]{1,0:T(1,128)} %bitcast.13), custom_call_target="tpu_custom_call" | custom-call | tf_op jit(solution)/shard_map/travel/pallas_call | solution.py:339
  82.5 0.0 copy-done
  82.5 4.8 %settle.1 = (f32[254,16,128]{2,1,0:T(8,128)}, f32[4,256,1024]{2,1,0:T(8,128)}) custom-call(f32[288,16,128]{2,1,0:T(8,128)} %bitcast.10, f32[254,16,128]{2,1,0:T(8,128)S(1)} %bitcast.9, f32[4,256,1024]{2,1,0:T(8,128)} %get-tuple-element.7.field_hbm), custom_call_target="tpu_custom_call" | custom-call | tf_op jit(solution)/shard_map/settle/pallas_call | solution.py:375
Async XLA Ops:
  0.6 81.9 %copy-start = (f32[2,127,16,128]{3,2,1,0:T(8,128)S(1)}, f32[2,127,16,128]{3,2,1,0:T(8,128)}, u32[]{:S(2)}) copy-start(f32[2,127,16,128]{3,2,1,0:T(8,128)} %param.6) | copy-start | bytes 6242308
